TPU v7x, 128 devices: a whole 4x4x4 slice. The times are simulated.
128 devices in a mesh: row: 32 (over z, y, x_hi), col: 4 (over x_lo, core).
Axes of the slice: x: 4 (x_hi: 2, x_lo: 2; x = x_hi * 2 + x_lo), y: 4, z: 4, core: 2. Of those that a mesh axis runs over, the one named last changes fastest.
Arguments:
- source: bfloat16 [64, 32768], P(None, ('row', 'col')), may hold values from -1 to 1
- target: bfloat16 [64, 98304], P(None, ('col', 'row')), may hold values from -1 to 1
- source_logw: float32 [32768], P('row'), may hold values from -3 to 0
- target_logw: float32 [98304], P(('col', 'row')), may hold values from -3 to 0
- start_potential: bfloat16 [1, 98304], P(None, ('col', 'row')), may hold values from -1 to 12
Outputs:
- row_potential: float32 [32768], P('row')
- col_potential: float32 [98304], P(('col', 'row'))
All inputs are finite; a program needn't handle non-finite values.
Results may differ from a plain program's by a relative error of at most 0.0015.
Values may be sent and summed in bfloat16 or wider, within the bound.
No kernel may reach another device: no remote copies, remote signals or barrier semaphores. Data moves between devices by JAX's collectives and lax.ppermute only.
A program may use at most 64 MiB of HBM per device.

v0:
```python
import functools
import math

import jax
import jax.numpy as jnp
from jax import lax
from jax.experimental import pallas as pl
from jax.experimental.pallas import tpu as pltpu
from jax.sharding import Mesh
from jax.sharding import PartitionSpec as P

smoothing = 0.1
log2e = math.log2(math.e)
kappa = 2.0 * log2e / smoothing
scale = log2e / smoothing
dim = 64
headroom = 24.0
sample = 128
row_blocks = (1024, 1024)
column_blocks = (1024, 768)
largest = 3e38
shape = (4, 4, 2, 2, 2)
names = ("z", "y", "xh", "xl", "core")
x = ("xh", "xl")


def three_parts(v):
    hi = v.astype(jnp.bfloat16).astype(jnp.float32)
    mid = (v - hi).astype(jnp.bfloat16).astype(jnp.float32)
    return hi, mid, v - hi - mid


def rounded(v):
    return v.astype(jnp.bfloat16).astype(jnp.float32)


def log_add(a, b):
    top = jnp.maximum(a, b)
    return top + jnp.log2(1.0 + jnp.exp2(-jnp.abs(a - b)))


def streamed_features(points, bias):
    m = points.shape[1]
    hi, mid, lo = three_parts(bias)
    row = lax.broadcasted_iota(jnp.int32, (16, m), 0)
    extra = jnp.where(row == 0, hi, jnp.where(row == 1, mid, jnp.where(row == 2, lo, 0.0)))
    extra = jnp.where(row == 3, 1.0, extra).astype(jnp.bfloat16)
    block = jnp.concatenate([points, extra, jnp.zeros((48, m), jnp.bfloat16)], axis=0)
    return block.T


def fill_held(held_ref, start, points):
    cols = slice(start, start + points.shape[1])
    wide = points.astype(jnp.float32) * kappa
    hi = wide.astype(jnp.bfloat16)
    held_ref[:dim, cols] = hi
    held_ref[dim:, cols] = (wide - hi.astype(jnp.float32)).astype(jnp.bfloat16)


class LogSums:
    def __init__(self, stream_ref, held_ref, extra_ref, out_ref, shift_ref, blocks):
        self.stream_ref, self.held_ref, self.extra_ref = stream_ref, held_ref, extra_ref
        self.out_ref, self.shift_ref = out_ref, shift_ref
        self.chunk, self.tile = blocks
        self.m, self.n = stream_ref.shape[0], held_ref.shape[1]

    def scores(self, start, size, cols):
        u = self.stream_ref[pl.ds(start, size), :]
        held = self.held_ref[:, cols]
        zeros = jnp.zeros((dim, held.shape[1]), jnp.bfloat16)
        held = jnp.concatenate(
            [held[:dim], self.extra_ref[:, cols], zeros[:48], held[dim:], zeros], axis=0
        )
        return lax.dot_general(
            jnp.concatenate([u, u], axis=1),
            held,
            (((1,), (0,)), ((), ())),
            preferred_element_type=jnp.float32,
        )

    def set_extra(self, shift):
        row = lax.broadcasted_iota(jnp.int32, (16, self.n), 0)
        extra = jnp.where(row < 3, 1.0, jnp.where(row == 3, -shift, 0.0))
        self.extra_ref[...] = extra.astype(jnp.bfloat16)

    def tiles(self, step):
        def body(t, _):
            step(pl.ds(pl.multiple_of(t * self.tile, self.tile), self.tile))
            return 0

        lax.fori_loop(0, self.n // self.tile, body, 0)

    def estimate(self):
        self.set_extra(jnp.zeros((1, self.n), jnp.float32))
        top = jnp.max(self.scores(0, sample, slice(None)), axis=0, keepdims=True)
        self.shift_ref[...] = rounded(top + headroom)

    def sums(self):
        self.set_extra(self.shift_ref[...])

        def add_up(cols):
            acc = jnp.zeros((8, self.tile), jnp.float32)
            for c in range(self.m // self.chunk):
                e = jnp.exp2(self.scores(c * self.chunk, self.chunk, cols))
                acc = acc + jnp.sum(e.reshape(self.chunk // 8, 8, self.tile), axis=0)
            self.out_ref[:, cols] = jnp.sum(acc, axis=0, keepdims=True)

        self.tiles(add_up)
        return self.out_ref[...]

    def exact(self):
        self.set_extra(jnp.zeros((1, self.n), jnp.float32))

        def highest(cols):
            def step(c, acc):
                v = self.scores(pl.multiple_of(c * sample, sample), sample, cols)
                return jnp.maximum(acc, jnp.max(v, axis=0, keepdims=True))

            none = jnp.full((1, self.tile), -largest, jnp.float32)
            self.out_ref[:, cols] = lax.fori_loop(0, self.m // sample, step, none)

        self.tiles(highest)
        return self.out_ref[...]

    def run(self, prior=None):
        if prior is None:
            self.estimate()

        def attempt(state):
            total = self.sums()
            if prior is not None:
                total = total + jnp.exp2(prior - self.shift_ref[...])
            again = jnp.logical_not(jnp.max(total) < largest)
            self.out_ref[...] = self.shift_ref[...] + jnp.log2(total)

            @pl.when(again)
            def _():
                top = self.exact()
                self.shift_ref[...] = rounded(top if prior is None else jnp.maximum(top, prior))

            return state[0] + 1, again

        lax.while_loop(lambda s: jnp.logical_and(s[1], s[0] < 2), attempt, (0, True))


def fill_row_stream(t_ref, stream_ref):
    pieces, _, width = t_ref.shape
    for k in range(pieces):
        points = t_ref[k, :dim, :]
        lifted = t_ref[k, dim : dim + 1, :].astype(jnp.float32)
        wide = points.astype(jnp.float32)
        bias = scale * (lifted - jnp.sum(wide * wide, axis=0, keepdims=True))
        stream_ref[k * width : (k + 1) * width, :] = streamed_features(points, bias)


def first_row_kernel(t_ref, s_ref, out_ref, held_ref, shift_ref, stream_ref, extra_ref):
    fill_row_stream(t_ref, stream_ref)
    for k in range(s_ref.shape[0]):
        fill_held(held_ref, k * s_ref.shape[2], s_ref[k, :dim, :])
    LogSums(stream_ref, held_ref, extra_ref, out_ref, shift_ref, row_blocks).run()


def next_row_kernel(t_ref, held_ref, old_ref, prior_ref, out_ref, stream_ref, extra_ref, shift_ref):
    fill_row_stream(t_ref, stream_ref)
    shift_ref[...] = old_ref[...]
    LogSums(stream_ref, held_ref, extra_ref, out_ref, shift_ref, row_blocks).run(prior_ref[...])


def fill_column_stream(s_ref, lse_ref, received_ref, logw_ref, place_ref, stream_ref):
    pieces, _, width = s_ref.shape
    n = lse_ref.shape[1]
    half = logw_ref.shape[1]
    here, there = logw_ref[...], received_ref[:, n:]
    ordered = place_ref[0] == 0
    logw = (jnp.where(ordered, here, there), jnp.where(ordered, there, here))
    for k in range(pieces):
        core, hi, lo, xl = k // 8, k // 4 % 2, k // 2 % 2, k % 2
        at = lo * (half // 2) + (2 * xl + core) * width
        cols = slice(k * width, (k + 1) * width)
        lse = log_add(lse_ref[:, cols], received_ref[:, cols])
        bias = log2e * logw[hi][:, at : at + width] - lse
        stream_ref[cols, :] = streamed_features(s_ref[k], bias)


def columns(first, t_ref, out_ref, stream_ref, held_ref, extra_ref, shift_ref):
    width = t_ref.shape[2]
    for k in range(held_ref.shape[1] // width):
        fill_held(held_ref, k * width, t_ref[first + k, :dim, :])
    LogSums(stream_ref, held_ref, extra_ref, out_ref, shift_ref, column_blocks).run()


def first_column_kernel(*refs):
    ins, (t_ref, out_ref, stream_ref), scratch = refs[:-6], refs[-6:-3], refs[-3:]
    fill_column_stream(*ins, stream_ref)
    columns(0, t_ref, out_ref, stream_ref, *scratch)


def next_column_kernel(first, stream_ref, t_ref, out_ref, *scratch):
    columns(first, t_ref, out_ref, stream_ref, *scratch)


whole = pl.BlockSpec(memory_space=pltpu.VMEM)
scalar = pl.BlockSpec(memory_space=pltpu.SMEM)


def call(kernel, name, operands, outs, scratch, in_specs=None):
    return pl.pallas_call(
        kernel,
        in_specs=in_specs or [whole] * len(operands),
        out_specs=[whole] * len(outs),
        out_shape=[jax.ShapeDtypeStruct(*o) for o in outs],
        scratch_shapes=[pltpu.VMEM(*s) for s in scratch],
        compiler_params=pltpu.CompilerParams(vmem_limit_bytes=40 * 2**20),
        name=name,
    )(*operands)


def stream_of(points):
    return ((points, 128), jnp.bfloat16)


def arrays_of(n):
    row = ((1, n), jnp.float32)
    return row, ((2 * dim, n), jnp.bfloat16), ((16, n), jnp.bfloat16)


def points_of(targets):
    return targets.shape[0] * targets.shape[2]


def first_row_sums(targets, sources):
    row, held, extra = arrays_of(points_of(sources))
    outs = (row, held, row)
    scratch = (stream_of(points_of(targets)), extra)
    return call(first_row_kernel, "first_row_sums", (targets, sources), outs, scratch)


def next_row_sums(targets, prior, held, shift):
    row, _, extra = arrays_of(held.shape[1])
    scratch = (stream_of(points_of(targets)), extra, row)
    return call(next_row_kernel, "next_row_sums", (targets, held, shift, prior), (row,), scratch)[0]


def first_column_sums(targets, sources, *more):
    row, held, extra = arrays_of(points_of(targets))
    operands = (sources, *more, targets)
    specs = [scalar if v.dtype == jnp.int32 else whole for v in operands]
    outs = (row, stream_of(points_of(sources)))
    return call(first_column_kernel, "first_column_sums", operands, outs, (held, extra, row), specs)


def next_column_sums(stream, targets, first, count):
    row, held, extra = arrays_of(count * targets.shape[2])
    kernel = functools.partial(next_column_kernel, first)
    return call(kernel, "next_column_sums", (stream, targets), (row,), (held, extra, row))[0]


def exchange(v, axes, flip):
    size = lax.axis_size(axes)
    return lax.ppermute(v, axes, [(i, i ^ flip) for i in range(size)])


def in_order(bit, v, other):
    first = bit == 0
    return jnp.concatenate([jnp.where(first, v, other), jnp.where(first, other, v)], axis=0)


def doubled(v, axes, flip, bit):
    return in_order(bit, v, exchange(v, axes, flip))


def norms(points):
    wide = points.astype(jnp.float32)
    return jnp.sum(wide * wide, axis=0)


def per_device(source, target, source_logw, target_logw, start_potential):
    z, y, xh, xl, core = (lax.axis_index(name) for name in names)
    width, span = source.shape[1], target.shape[1]

    sources = source[None]
    targets = jnp.concatenate([target, start_potential], axis=0)[None]
    sources = doubled(sources, x, 1, xl)
    targets = jnp.concatenate([targets, exchange(targets, x, 3)], axis=0)
    sources = doubled(sources, "z", 1, z % 2)
    targets = jnp.concatenate([targets, exchange(targets, "y", 1)], axis=0)
    sources = doubled(sources, "z", 3, z // 2)
    sources = doubled(sources, "core", 1, core)
    others = exchange(targets, "y", 3)

    lse, held, shift = first_row_sums(targets, sources)
    lse = next_row_sums(others, lse, held, shift)
    lse = log_add(lse, exchange(lse, "core", 1))
    lse = log_add(lse, exchange(lse, x, 1))
    count = lse.shape[1]
    logw = source_logw[None]
    received = exchange(jnp.concatenate([lse, logw], axis=1), "z", 1)
    lse = log_add(lse, received[:, :count])
    received = received[:, count:]
    logw = jnp.where(z % 2 == 0, jnp.concatenate([logw, received], axis=1), jnp.concatenate([received, logw], axis=1))
    received = exchange(jnp.concatenate([lse, logw], axis=1), "z", 3)
    place = (z // 2).astype(jnp.int32).reshape(1)
    partial, stream = first_column_sums(others, sources, lse, received, logw, place)

    sent = exchange(partial, "y", 3)
    half = 2 * span
    partial = next_column_sums(stream, targets, 2, 2)
    partial = log_add(partial, sent[:, half:])
    sent = log_add(exchange(partial, "y", 1), sent[:, :half])
    partial = log_add(next_column_sums(stream, targets, 0, 2), sent)[0]
    partial = log_add(partial[:span], exchange(partial[span:], x, 3))

    lse = log_add(lse, received[:, : lse.shape[1]])
    mine = lax.dynamic_index_in_dim(lse.reshape(2, 4, 2, width), z, 1, False)
    mine = mine.transpose(1, 0, 2).reshape(4 * width)
    picked = sources[:, :dim, :].reshape(2, 4, 2, dim, width)
    picked = lax.dynamic_index_in_dim(picked, z, 1, False)
    row_sq = jnp.sum(jnp.square(picked.astype(jnp.float32)), axis=2)
    row_sq = row_sq.transpose(1, 0, 2).reshape(4 * width)
    row_lse = mine / log2e - row_sq / smoothing
    row_potential = smoothing * source_logw - smoothing * row_lse

    col_lse = partial / log2e - norms(target) / smoothing
    col_potential = smoothing * target_logw - smoothing * col_lse
    return (row_potential, col_potential)


def solution(mesh):
    devices = Mesh(mesh.devices.reshape(shape), names)
    rows = ("z", "y", "xh")
    columns_over = ("xl", "core", "z", "y", "xh")
    in_specs = (P(None, names), P(None, columns_over), P(rows), P(columns_over), P(None, columns_over))
    out_specs = (P(rows), P(columns_over))
    return jax.shard_map(
        per_device, mesh=devices, in_specs=in_specs, out_specs=out_specs, check_vma=False
    )
```

profile of v0, /device:TPU:24, one launch (start us, length us, event | category | flops | bytes accessed | tf_op | source)
XLA Modules:
  0.0 176.3 jit_solution(1860320478942823387)
XLA Ops:
  0.6 1.6 collective-permute-start.3
  2.2 2.6 %collective-permute-done.3 = bf16[1,64,256]{2,1,0:T(8,128)(2,1)S(1)} collective-permute-done((bf16[1,64,256]{2,1,0:T(8,128)(2,1)}, bf16[1,64,256]{2,1,0:T(8,128)(2,1)S(1)}, u32[]{:S(2)}, u32[]{:S(2)}) %collective-permute-start.3) | collective-permute-done | bytes 32800 | tf_op jit(solution)/shard_map/ppermute | solution.py:260
  4.8 0.8 broadcast_select_fusion.7
  5.6 0.0 copy-start
  5.6 0.0 copy-start.3
  5.6 2.0 %collective-permute-start.4 = (bf16[2,64,256]{2,1,0:T(8,128)(2,1)S(1)}, bf16[2,64,256]{2,1,0:T(8,128)(2,1)S(1)}, u32[]{:S(2)}, u32[]{:S(2)}) collective-permute-start(bf16[2,64,256]{2,1,0:T(8,128)(2,1)S(1)} %pad_maximum_fusion.5), channel_id=1, source_target_pairs={{0,32},{32,0},{64,96},{96,64},{1,33},{33,1},{65,97},{97,65},{2,34}... | collective-permute-start | bytes 196616 | tf_op jit(solution)/shard_map/ppermute | solution.py:260
  7.6 0.0 copy-done
  7.6 0.0 copy-done.3
  7.7 2.8 %collective-permute-start = (bf16[1,65,768]{2,1,0:T(8,128)(2,1)S(1)}, bf16[1,65,768]{2,1,0:T(8,128)(2,1)S(1)}, u32[]{:S(2)}, u32[]{:S(2)}) collective-permute-start(bf16[1,65,768]{2,1,0:T(8,128)(2,1)S(1)} %maximum_bitcast_fusion), channel_id=1, source_target_pairs={{0,6},{2,4},{4,2},{6,0},{1,7},{3,5},{5,3},{7,1},{8,14},{10,12},{12... | collective-permute-start | bytes 299528 | tf_op jit(solution)/shard_map/ppermute | solution.py:260
  10.5 0.0 collective-permute-done.4
  10.5 3.6 %collective-permute-start.5 = (bf16[4,64,256]{2,1,0:T(8,128)(2,1)S(1)}, bf16[4,64,256]{2,1,0:T(8,128)(2,1)S(1)}, u32[]{:S(2)}, u32[]{:S(2)}) collective-permute-start(bf16[4,64,256]{2,1,0:T(8,128)(2,1)S(1)} %pad_maximum_fusion.4), channel_id=1, source_target_pairs={{0,96},{32,64},{64,32},{96,0},{1,97},{33,65},{65,33},{97,1},{2,98}... | collective-permute-start | bytes 393224 | tf_op jit(solution)/shard_map/ppermute | solution.py:260
  14.1 0.0 collective-permute-done
  14.2 0.8 collective-permute-start.1
  15.0 2.1 %collective-permute-done.5 = bf16[4,64,256]{2,1,0:T(8,128)(2,1)S(1)} collective-permute-done((bf16[4,64,256]{2,1,0:T(8,128)(2,1)S(1)}, bf16[4,64,256]{2,1,0:T(8,128)(2,1)S(1)}, u32[]{:S(2)}, u32[]{:S(2)}) %collective-permute-start.5) | collective-permute-done | bytes 131104 | tf_op jit(solution)/shard_map/ppermute | solution.py:260
  17.1 0.1 collective-permute-start.6
  17.2 2.9 %collective-permute-done.1 = bf16[2,65,768]{2,1,0:T(8,128)(2,1)S(1)} collective-permute-done((bf16[2,65,768]{2,1,0:T(8,128)(2,1)S(1)}, bf16[2,65,768]{2,1,0:T(8,128)(2,1)S(1)}, u32[]{:S(2)}, u32[]{:S(2)}) %collective-permute-start.1) | collective-permute-done | bytes 199712 | tf_op jit(solution)/shard_map/ppermute | solution.py:260
  20.2 0.3 collective-permute-start.2
  20.5 0.0 collective-permute-done.6
  20.6 38.0 %first_row_sums.1 = (f32[1,4096]{1,0:T(1,128)S(1)}, bf16[128,4096]{1,0:T(8,128)(2,1)S(1)}, f32[1,4096]{1,0:T(1,128)S(1)}) custom-call(bf16[4,65,768]{2,1,0:T(8,128)(2,1)S(1)} %pad_maximum_fusion.1.t_ref, bf16[16,64,256]{2,1,0:T(8,128)(2,1)S(1)} %pad_maximum_fusion.s_ref.refs_0_), custom_call_target="tpu_custom_call" | custom-call | tf_op jit(solution)/shard_map/first_row_sums/pallas_call | solution.py:207
  58.6 0.0 collective-permute-done.2.t_ref.refs_5_
  58.6 7.6 %next_row_sums.1 = f32[1,4096]{1,0:T(1,128)S(1)} custom-call(bf16[4,65,768]{2,1,0:T(8,128)(2,1)S(1)} %collective-permute-done.2.t_ref.refs_5_, bf16[128,4096]{1,0:T(8,128)(2,1)S(1)} %get-tuple-element.7.held_ref, f32[1,4096]{1,0:T(1,128)S(1)} %get-tuple-element.8.old_ref, f32[1,4096]{1,0:T(1,128)S(1)} %get-tuple-element.9.prior_ref), custom_call_target="tpu_custom_call" | custom-call | tf_op jit(solution)/shard_map/next_row_sums/pallas_call | solution.py:207
  66.3 0.1 collective-permute-start.7
  66.4 1.2 collective-permute-done.7
  67.5 0.1 multiply_add_fusion.2
  67.6 1.6 collective-permute-start.8
  69.2 2.2 %collective-permute-done.8 = f32[1,4096]{1,0:T(1,128)S(1)} collective-permute-done((f32[1,4096]{1,0:T(1,128)S(1)}, f32[1,4096]{1,0:T(1,128)S(1)}, u32[]{:S(2)}, u32[]{:S(2)}) %collective-permute-start.8) | collective-permute-done | bytes 16416 | tf_op jit(solution)/shard_map/ppermute | solution.py:260
  71.4 0.1 multiply_add_fusion.1
  71.5 0.0 copy-done.1
  71.5 0.4 collective-permute-start.9
  71.9 3.5 %collective-permute-done.9 = f32[1,5120]{1,0:T(1,128)S(1)} collective-permute-done((f32[1,5120]{1,0:T(1,128)S(1)}, f32[1,5120]{1,0:T(1,128)S(1)}, u32[]{:S(2)}, u32[]{:S(2)}) %collective-permute-start.9) | collective-permute-done | bytes 20512 | tf_op jit(solution)/shard_map/ppermute | solution.py:260
  75.4 0.1 multiply_add_fusion.refs_1_
  75.5 2.5 %collective-permute-start.10 = (f32[1,6144]{1,0:T(1,128)S(1)}, f32[1,6144]{1,0:T(1,128)S(1)}, u32[]{:S(2)}, u32[]{:S(2)}) collective-permute-start(f32[1,6144]{1,0:T(1,128)S(1)} %pad_maximum_fusion.6), channel_id=1, source_target_pairs={{0,96},{32,64},{64,32},{96,0},{1,97},{33,65},{65,33},{97,1},{2,98}... | collective-permute-start | bytes 73736 | tf_op jit(solution)/shard_map/ppermute | solution.py:260
  78.1 2.5 %collective-permute-done.10.refs_2_ = f32[1,6144]{1,0:T(1,128)S(1)} collective-permute-done((f32[1,6144]{1,0:T(1,128)S(1)}, f32[1,6144]{1,0:T(1,128)S(1)}, u32[]{:S(2)}, u32[]{:S(2)}) %collective-permute-start.10) | collective-permute-done | bytes 24608 | tf_op jit(solution)/shard_map/ppermute | solution.py:260
  80.6 43.3 %first_column_sums.1 = (f32[1,3072]{1,0:T(1,128)S(1)}, bf16[4096,128]{1,0:T(8,128)(2,1)S(1)}) custom-call(bf16[16,64,256]{2,1,0:T(8,128)(2,1)S(1)} %pad_maximum_fusion.s_ref.refs_0_, f32[1,4096]{1,0:T(1,128)S(1)} %multiply_add_fusion.refs_1_, f32[1,6144]{1,0:T(1,128)S(1)} %collective-permute-done.10.refs_2_, f32[1,2048]{1,0:T(1,128)S(1)} %broadcast_select_fusion.8.refs_3_, ...), custom_call_target="tpu_custom_call" | custom-call | tf_op jit(solution)/shard_map/first_column_sums/pallas_call | solution.py:207
  123.9 0.3 collective-permute-start.11
  124.2 0.1 add_reduce_fusion
  124.3 4.0 %next_column_sums.3 = f32[1,1536]{1,0:T(1,128)S(1)} custom-call(bf16[4096,128]{1,0:T(8,128)(2,1)S(1)} %get-tuple-element.10.stream_ref, bf16[4,65,768]{2,1,0:T(8,128)(2,1)S(1)} %pad_maximum_fusion.1.t_ref), custom_call_target="tpu_custom_call" | custom-call | tf_op jit(solution)/shard_map/next_column_sums/pallas_call | solution.py:207
  128.4 0.7 collective-permute-done.11
  129.1 0.1 collective-permute-start.12
  129.2 4.0 %next_column_sums.2 = f32[1,1536]{1,0:T(1,128)S(1)} custom-call(bf16[4096,128]{1,0:T(8,128)(2,1)S(1)} %get-tuple-element.10.stream_ref, bf16[4,65,768]{2,1,0:T(8,128)(2,1)S(1)} %pad_maximum_fusion.1.t_ref), custom_call_target="tpu_custom_call" | custom-call | tf_op jit(solution)/shard_map/next_column_sums/pallas_call | solution.py:207
  133.3 0.0 collective-permute-done.12
  133.3 0.1 multiply_add_fusion.3
  133.4 40.7 %collective-permute-start.13 = (f32[768]{0:T(1024)S(1)}, f32[768]{0:T(1024)S(1)}, u32[]{:S(2)}, u32[]{:S(2)}) collective-permute-start(f32[768]{0:T(1024)S(1)} %get-tuple-element.12), channel_id=1, source_target_pairs={{0,6},{2,4},{4,2},{6,0},{1,7},{3,5},{5,3},{7,1},{8,14},{10,12},{12... | collective-permute-start | bytes 9224 | tf_op jit(solution)/shard_map/ppermute | solution.py:260
  174.1 0.0 copy-start.2
  174.1 0.6 multiply_subtract_fusion.1
  174.7 1.0 collective-permute-done.13
  175.7 0.0 copy-done.2
  175.7 0.6 multiply_subtract_fusion
  (23 shorter events, 0.5 us)
Async XLA Ops:
  0.6 4.2 %collective-permute-start.3 = (bf16[1,64,256]{2,1,0:T(8,128)(2,1)}, bf16[1,64,256]{2,1,0:T(8,128)(2,1)S(1)}, u32[]{:S(2)}, u32[]{:S(2)}) collective-permute-start(bf16[1,64,256]{2,1,0:T(8,128)(2,1)} %bitcast.35), channel_id=1, source_target_pairs={{0,2},{2,0},{4,6},{6,4},{1,3},{3,1},{5,7},{7,5},{8,10},{10,8},{12,... | collective-permute-start | bytes 98312 | tf_op jit(solution)/shard_map/ppermute | solution.py:260
  5.6 2.0 %copy-start = (bf16[64,768]{1,0:T(8,128)(2,1)S(1)}, bf16[64,768]{1,0:T(8,128)(2,1)}, u32[]{:S(2)}) copy-start(bf16[64,768]{1,0:T(8,128)(2,1)} %param.6) | copy-start | bytes 294916
  5.6 2.0 %copy-start.3 = (bf16[1,768]{1,0:T(2,128)(2,1)S(1)}, bf16[1,768]{1,0:T(2,128)(2,1)}, u32[]{:S(2)}) copy-start(bf16[1,768]{1,0:T(2,128)(2,1)} %param.9) | copy-start | bytes 4612
  5.6 4.9 %collective-permute-start.4 = (bf16[2,64,256]{2,1,0:T(8,128)(2,1)S(1)}, bf16[2,64,256]{2,1,0:T(8,128)(2,1)S(1)}, u32[]{:S(2)}, u32[]{:S(2)}) collective-permute-start(bf16[2,64,256]{2,1,0:T(8,128)(2,1)S(1)} %pad_maximum_fusion.5), channel_id=1, source_target_pairs={{0,32},{32,0},{64,96},{96,64},{1,33},{33,1},{65,97},{97,65},{2,34}... | collective-permute-start | bytes 196616 | tf_op jit(solution)/shard_map/ppermute | solution.py:260
  7.7 6.5 %collective-permute-start = (bf16[1,65,768]{2,1,0:T(8,128)(2,1)S(1)}, bf16[1,65,768]{2,1,0:T(8,128)(2,1)S(1)}, u32[]{:S(2)}, u32[]{:S(2)}) collective-permute-start(bf16[1,65,768]{2,1,0:T(8,128)(2,1)S(1)} %maximum_bitcast_fusion), channel_id=1, source_target_pairs={{0,6},{2,4},{4,2},{6,0},{1,7},{3,5},{5,3},{7,1},{8,14},{10,12},{12... | collective-permute-start | bytes 299528 | tf_op jit(solution)/shard_map/ppermute | solution.py:260
  10.5 6.6 %collective-permute-start.5 = (bf16[4,64,256]{2,1,0:T(8,128)(2,1)S(1)}, bf16[4,64,256]{2,1,0:T(8,128)(2,1)S(1)}, u32[]{:S(2)}, u32[]{:S(2)}) collective-permute-start(bf16[4,64,256]{2,1,0:T(8,128)(2,1)S(1)} %pad_maximum_fusion.4), channel_id=1, source_target_pairs={{0,96},{32,64},{64,32},{96,0},{1,97},{33,65},{65,33},{97,1},{2,98}... | collective-permute-start | bytes 393224 | tf_op jit(solution)/shard_map/ppermute | solution.py:260
  14.2 6.0 %collective-permute-start.1 = (bf16[2,65,768]{2,1,0:T(8,128)(2,1)S(1)}, bf16[2,65,768]{2,1,0:T(8,128)(2,1)S(1)}, u32[]{:S(2)}, u32[]{:S(2)}) collective-permute-start(bf16[2,65,768]{2,1,0:T(8,128)(2,1)S(1)} %pad_maximum_fusion.3), channel_id=1, source_target_pairs={{0,8},{8,0},{16,24},{24,16},{1,9},{9,1},{17,25},{25,17},{2,10},{10... | collective-permute-start | bytes 599048 | tf_op jit(solution)/shard_map/ppermute | solution.py:260
  17.1 3.4 %collective-permute-start.6 = (bf16[8,64,256]{2,1,0:T(8,128)(2,1)S(1)}, bf16[8,64,256]{2,1,0:T(8,128)(2,1)S(1)}, u32[]{:S(2)}, u32[]{:S(2)}) collective-permute-start(bf16[8,64,256]{2,1,0:T(8,128)(2,1)S(1)} %pad_maximum_fusion.2), channel_id=1, source_target_pairs={{0,1},{1,0},{2,3},{3,2},{4,5},{5,4},{6,7},{7,6},{8,9},{9,8},{10,11... | collective-permute-start | bytes 786440 | tf_op jit(solution)/shard_map/ppermute | solution.py:260
  20.2 38.4 %collective-permute-start.2 = (bf16[4,65,768]{2,1,0:T(8,128)(2,1)S(1)}, bf16[4,65,768]{2,1,0:T(8,128)(2,1)S(1)}, u32[]{:S(2)}, u32[]{:S(2)}) collective-permute-start(bf16[4,65,768]{2,1,0:T(8,128)(2,1)S(1)} %pad_maximum_fusion.1.t_ref), channel_id=1, source_target_pairs={{0,24},{8,16},{16,8},{24,0},{1,25},{9,17},{17,9},{25,1},{2,26},{10... | collective-permute-start | bytes 1198088 | tf_op jit(solution)/shard_map/ppermute | solution.py:260
  66.3 1.3 collective-permute-start.7
  67.5 4.0 %copy-start.1 = (f32[1024]{0:T(1024)S(1)}, f32[1024]{0:T(1024)}, u32[]{:S(2)}) copy-start(f32[1024]{0:T(1024)} %param.7) | copy-start | bytes 12292
  67.6 3.8 %collective-permute-start.8 = (f32[1,4096]{1,0:T(1,128)S(1)}, f32[1,4096]{1,0:T(1,128)S(1)}, u32[]{:S(2)}, u32[]{:S(2)}) collective-permute-start(f32[1,4096]{1,0:T(1,128)S(1)} %multiply_add_fusion.2), channel_id=1, source_target_pairs={{0,2},{2,0},{4,6},{6,4},{1,3},{3,1},{5,7},{7,5},{8,10},{10,8},{12,... | collective-permute-start | bytes 49160 | tf_op jit(solution)/shard_map/ppermute | solution.py:260
  71.5 3.9 %collective-permute-start.9 = (f32[1,5120]{1,0:T(1,128)S(1)}, f32[1,5120]{1,0:T(1,128)S(1)}, u32[]{:S(2)}, u32[]{:S(2)}) collective-permute-start(f32[1,5120]{1,0:T(1,128)S(1)} %pad_maximum_fusion.7), channel_id=1, source_target_pairs={{0,32},{32,0},{64,96},{96,64},{1,33},{33,1},{65,97},{97,65},{2,34}... | collective-permute-start | bytes 61448 | tf_op jit(solution)/shard_map/ppermute | solution.py:260
  75.5 5.1 %collective-permute-start.10 = (f32[1,6144]{1,0:T(1,128)S(1)}, f32[1,6144]{1,0:T(1,128)S(1)}, u32[]{:S(2)}, u32[]{:S(2)}) collective-permute-start(f32[1,6144]{1,0:T(1,128)S(1)} %pad_maximum_fusion.6), channel_id=1, source_target_pairs={{0,96},{32,64},{64,32},{96,0},{1,97},{33,65},{65,33},{97,1},{2,98}... | collective-permute-start | bytes 73736 | tf_op jit(solution)/shard_map/ppermute | solution.py:260
  123.9 5.2 %collective-permute-start.11 = (f32[1,3072]{1,0:T(1,128)S(1)}, f32[1,3072]{1,0:T(1,128)S(1)}, u32[]{:S(2)}, u32[]{:S(2)}) collective-permute-start(f32[1,3072]{1,0:T(1,128)S(1)} %get-tuple-element.11), channel_id=1, source_target_pairs={{0,24},{8,16},{16,8},{24,0},{1,25},{9,17},{17,9},{25,1},{2,26},{10... | collective-permute-start | bytes 36872 | tf_op jit(solution)/shard_map/ppermute | solution.py:260
  129.1 4.2 %collective-permute-start.12 = (f32[1,1536]{1,0:T(1,128)S(1)}, f32[1,1536]{1,0:T(1,128)S(1)}, u32[]{:S(2)}, u32[]{:S(2)}) collective-permute-start(f32[1,1536]{1,0:T(1,128)S(1)} %multiply_add_fusion.4), channel_id=1, source_target_pairs={{0,8},{8,0},{16,24},{24,16},{1,9},{9,1},{17,25},{25,17},{2,10},{10... | collective-permute-start | bytes 18440 | tf_op jit(solution)/shard_map/ppermute | solution.py:260
  133.4 42.3 %collective-permute-start.13 = (f32[768]{0:T(1024)S(1)}, f32[768]{0:T(1024)S(1)}, u32[]{:S(2)}, u32[]{:S(2)}) collective-permute-start(f32[768]{0:T(1024)S(1)} %get-tuple-element.12), channel_id=1, source_target_pairs={{0,6},{2,4},{4,2},{6,0},{1,7},{3,5},{5,3},{7,1},{8,14},{10,12},{12... | collective-permute-start | bytes 9224 | tf_op jit(solution)/shard_map/ppermute | solution.py:260
  174.1 1.6 copy-start.2
where the time goes:
time: 175 us; the launch traced here: 176 us
  Pallas kernels  97 us (55%)
  starting transfers between devices  56.8 us (32%)
  waiting for transfers between devices  18.8 us (11%)
  other arithmetic  2.76 us (2%)
    pallas_call x5, Pallas kernels, call(): pl.pallas_call(kernel, in_specs=in_specs or [whole] * len(operands), out_...  97 us
    ppermute x14, starting transfers between devices, exchange(): return lax.ppermute(v, axes, [(i, i ^ flip) for i in range(size)])  56.8 us
    ppermute x14, waiting for transfers between devices, exchange(): return lax.ppermute(v, axes, [(i, i ^ flip) for i in range(size)])  18.8 us
  transfers between devices with their start and end apart: 14, of which 9 were waited for; matrix products, arithmetic and copies ran while one was open for 1% of the time, Pallas kernels for 26%

commit v1 on v0

--- a/solution.py
+++ b/solution.py
@@ -63,6 +63,7 @@
         self.out_ref, self.shift_ref = out_ref, shift_ref
         self.chunk, self.tile = blocks
         self.m, self.n = stream_ref.shape[0], held_ref.shape[1]
+        self.unroll = 2 if self.n // self.tile % 2 == 0 and self.n > 2000 else 1
 
     def scores(self, start, size, cols):
         u = self.stream_ref[pl.ds(start, size), :]
@@ -88,7 +89,7 @@
             step(pl.ds(pl.multiple_of(t * self.tile, self.tile), self.tile))
             return 0
 
-        lax.fori_loop(0, self.n // self.tile, body, 0)
+        lax.fori_loop(0, self.n // self.tile, body, 0, unroll=self.unroll)
 
     def estimate(self):
         self.set_extra(jnp.zeros((1, self.n), jnp.float32))
@@ -280,13 +281,16 @@
 
     sources = source[None]
     targets = jnp.concatenate([target, start_potential], axis=0)[None]
-    sources = doubled(sources, x, 1, xl)
+    other = exchange(sources, x, 1)
+    sources = jnp.zeros((2, dim, width), sources.dtype)
+    sources = lax.dynamic_update_slice(sources, source[None], (xl, 0, 0))
+    sources = lax.dynamic_update_slice(sources, other, (1 - xl, 0, 0))
     targets = jnp.concatenate([targets, exchange(targets, x, 3)], axis=0)
     sources = doubled(sources, "z", 1, z % 2)
-    targets = jnp.concatenate([targets, exchange(targets, "y", 1)], axis=0)
+    targets = jnp.concatenate([targets, exchange(targets, "y", 3)], axis=0)
     sources = doubled(sources, "z", 3, z // 2)
     sources = doubled(sources, "core", 1, core)
-    others = exchange(targets, "y", 3)
+    others = exchange(targets, "y", 1)
 
     lse, held, shift = first_row_sums(targets, sources)
     lse = next_row_sums(others, lse, held, shift)
@@ -297,24 +301,33 @@
     received = exchange(jnp.concatenate([lse, logw], axis=1), "z", 1)
     lse = log_add(lse, received[:, :count])
     received = received[:, count:]
-    logw = jnp.where(z % 2 == 0, jnp.concatenate([logw, received], axis=1), jnp.concatenate([received, logw], axis=1))
+    logw = jnp.where(
+        z % 2 == 0,
+        jnp.concatenate([logw, received], axis=1),
+        jnp.concatenate([received, logw], axis=1),
+    )
     received = exchange(jnp.concatenate([lse, logw], axis=1), "z", 3)
     place = (z // 2).astype(jnp.int32).reshape(1)
     partial, stream = first_column_sums(others, sources, lse, received, logw, place)
 
-    sent = exchange(partial, "y", 3)
+    sent = exchange(partial, "y", 1)
     half = 2 * span
     partial = next_column_sums(stream, targets, 2, 2)
     partial = log_add(partial, sent[:, half:])
-    sent = log_add(exchange(partial, "y", 1), sent[:, :half])
-    partial = log_add(next_column_sums(stream, targets, 0, 2), sent)[0]
-    partial = log_add(partial[:span], exchange(partial[span:], x, 3))
-
+    more = exchange(partial, "y", 3)
+    partial = next_column_sums(stream, targets, 1, 1)
+    partial = log_add(log_add(partial, sent[:, span:half]), more[:, span:])
+    last = exchange(partial, x, 3)
+    partial = next_column_sums(stream, targets, 0, 1)
+    partial = log_add(log_add(partial, sent[:, :span]), more[:, :span])
+    partial = log_add(partial, last)[0]
+
+    at = 2 * (z // 2) + z % 2
     lse = log_add(lse, received[:, : lse.shape[1]])
-    mine = lax.dynamic_index_in_dim(lse.reshape(2, 4, 2, width), z, 1, False)
+    mine = lax.dynamic_index_in_dim(lse.reshape(2, 4, 2, width), at, 1, False)
     mine = mine.transpose(1, 0, 2).reshape(4 * width)
     picked = sources[:, :dim, :].reshape(2, 4, 2, dim, width)
-    picked = lax.dynamic_index_in_dim(picked, z, 1, False)
+    picked = lax.dynamic_index_in_dim(picked, at, 1, False)
     row_sq = jnp.sum(jnp.square(picked.astype(jnp.float32)), axis=2)
     row_sq = row_sq.transpose(1, 0, 2).reshape(4 * width)
     row_lse = mine / log2e - row_sq / smoothing

time: 175 us -> 158 us (0.903)
  the two profiles are of different devices: /device:TPU:24 before, /device:TPU:8 now
where the time goes in v1:
time: 158 us; the launch traced here: 155 us
  Pallas kernels  78.3 us (50%)
  starting transfers between devices  53.2 us (34%)
  waiting for transfers between devices  19.5 us (12%)
  other arithmetic  2.02 us (1%)
    pallas_call x6, Pallas kernels, call(): pl.pallas_call(kernel, in_specs=in_specs or [whole] * len(operands), out_...  78.3 us
    ppermute x14, starting transfers between devices, exchange(): return lax.ppermute(v, axes, [(i, i ^ flip) for i in range(size)])  53.2 us
    ppermute x14, waiting for transfers between devices, exchange(): return lax.ppermute(v, axes, [(i, i ^ flip) for i in range(size)])  19.5 us
  transfers between devices with their start and end apart: 14, of which 9 were waited for; matrix products, arithmetic and copies ran while one was open for 1% of the time, Pallas kernels for 41%

profile of v1, /device:TPU:8, one launch (start us, length us, event | category | flops | bytes accessed | tf_op | source)
XLA Modules:
  0.0 154.8 jit_solution(5147958616762549578)
XLA Ops:
  0.6 1.6 %collective-permute-start.3 = (bf16[1,64,256]{2,1,0:T(8,128)(2,1)}, bf16[1,64,256]{2,1,0:T(8,128)(2,1)S(1)}, u32[]{:S(2)}, u32[]{:S(2)}) collective-permute-start(bf16[1,64,256]{2,1,0:T(8,128)(2,1)} %bitcast.34), channel_id=1, source_target_pairs={{0,2},{2,0},{4,6},{6,4},{1,3},{3,1},{5,7},{7,5},{8,10},{10,8},{12,... | collective-permute-start | bytes 98312 | tf_op jit(solution)/shard_map/ppermute | solution.py:261
  2.2 0.0 copy-start
  2.2 0.8 copy-done.2
  3.0 1.8 %collective-permute-done.3 = bf16[1,64,256]{2,1,0:T(8,128)(2,1)S(1)} collective-permute-done((bf16[1,64,256]{2,1,0:T(8,128)(2,1)}, bf16[1,64,256]{2,1,0:T(8,128)(2,1)S(1)}, u32[]{:S(2)}, u32[]{:S(2)}) %collective-permute-start.3) | collective-permute-done | bytes 32800 | tf_op jit(solution)/shard_map/ppermute | solution.py:261
  4.8 1.9 %collective-permute-start.4 = (bf16[2,64,256]{2,1,0:T(8,128)(2,1)S(1)}, bf16[2,64,256]{2,1,0:T(8,128)(2,1)S(1)}, u32[]{:S(2)}, u32[]{:S(2)}) collective-permute-start(bf16[2,64,256]{2,1,0:T(8,128)(2,1)S(1)} %constant_dynamic-update-slice_fusion), channel_id=1, source_target_pairs={{0,32},{32,0},{64,96},{96,64},{1,33},{33,1},{65,97},{97,65},{2,34}... | collective-permute-start | bytes 196616 | tf_op jit(solution)/shard_map/ppermute | solution.py:261
  6.8 0.0 copy-done
  6.8 0.0 copy-done.4
  6.8 2.8 %collective-permute-start = (bf16[1,65,768]{2,1,0:T(8,128)(2,1)S(1)}, bf16[1,65,768]{2,1,0:T(8,128)(2,1)S(1)}, u32[]{:S(2)}, u32[]{:S(2)}) collective-permute-start(bf16[1,65,768]{2,1,0:T(8,128)(2,1)S(1)} %maximum_bitcast_fusion), channel_id=1, source_target_pairs={{0,6},{2,4},{4,2},{6,0},{1,7},{3,5},{5,3},{7,1},{8,14},{10,12},{12... | collective-permute-start | bytes 299528 | tf_op jit(solution)/shard_map/ppermute | solution.py:261
  9.6 0.0 collective-permute-done.4
  9.7 3.6 %collective-permute-start.5 = (bf16[4,64,256]{2,1,0:T(8,128)(2,1)S(1)}, bf16[4,64,256]{2,1,0:T(8,128)(2,1)S(1)}, u32[]{:S(2)}, u32[]{:S(2)}) collective-permute-start(bf16[4,64,256]{2,1,0:T(8,128)(2,1)S(1)} %pad_maximum_fusion.4), channel_id=1, source_target_pairs={{0,96},{32,64},{64,32},{96,0},{1,97},{33,65},{65,33},{97,1},{2,98}... | collective-permute-start | bytes 393224 | tf_op jit(solution)/shard_map/ppermute | solution.py:261
  13.3 0.0 collective-permute-done
  13.3 1.7 %collective-permute-start.1 = (bf16[2,65,768]{2,1,0:T(8,128)(2,1)S(1)}, bf16[2,65,768]{2,1,0:T(8,128)(2,1)S(1)}, u32[]{:S(2)}, u32[]{:S(2)}) collective-permute-start(bf16[2,65,768]{2,1,0:T(8,128)(2,1)S(1)} %pad_maximum_fusion.3), channel_id=1, source_target_pairs={{0,24},{8,16},{16,8},{24,0},{1,25},{9,17},{17,9},{25,1},{2,26},{10... | collective-permute-start | bytes 599048 | tf_op jit(solution)/shard_map/ppermute | solution.py:261
  14.9 1.3 collective-permute-done.5
  16.3 0.1 collective-permute-start.6
  16.4 2.9 %collective-permute-done.1 = bf16[2,65,768]{2,1,0:T(8,128)(2,1)S(1)} collective-permute-done((bf16[2,65,768]{2,1,0:T(8,128)(2,1)S(1)}, bf16[2,65,768]{2,1,0:T(8,128)(2,1)S(1)}, u32[]{:S(2)}, u32[]{:S(2)}) %collective-permute-start.1) | collective-permute-done | bytes 199712 | tf_op jit(solution)/shard_map/ppermute | solution.py:261
  19.4 1.7 %collective-permute-start.2 = (bf16[4,65,768]{2,1,0:T(8,128)(2,1)S(1)}, bf16[4,65,768]{2,1,0:T(8,128)(2,1)S(1)}, u32[]{:S(2)}, u32[]{:S(2)}) collective-permute-start(bf16[4,65,768]{2,1,0:T(8,128)(2,1)S(1)} %pad_maximum_fusion.1.t_ref), channel_id=1, source_target_pairs={{0,8},{8,0},{16,24},{24,16},{1,9},{9,1},{17,25},{25,17},{2,10},{10... | collective-permute-start | bytes 1198088 | tf_op jit(solution)/shard_map/ppermute | solution.py:261
  21.1 0.0 collective-permute-done.6
  21.2 37.3 %first_row_sums.1 = (f32[1,4096]{1,0:T(1,128)S(1)}, bf16[128,4096]{1,0:T(8,128)(2,1)S(1)}, f32[1,4096]{1,0:T(1,128)S(1)}) custom-call(bf16[4,65,768]{2,1,0:T(8,128)(2,1)S(1)} %pad_maximum_fusion.1.t_ref, bf16[16,64,256]{2,1,0:T(8,128)(2,1)S(1)} %pad_maximum_fusion.s_ref.refs_0_), custom_call_target="tpu_custom_call" | custom-call | tf_op jit(solution)/shard_map/first_row_sums/pallas_call | solution.py:208
  58.5 0.0 collective-permute-done.2.t_ref.refs_5_
  58.5 7.3 %next_row_sums.1 = f32[1,4096]{1,0:T(1,128)S(1)} custom-call(bf16[4,65,768]{2,1,0:T(8,128)(2,1)S(1)} %collective-permute-done.2.t_ref.refs_5_, bf16[128,4096]{1,0:T(8,128)(2,1)S(1)} %get-tuple-element.7.held_ref, f32[1,4096]{1,0:T(1,128)S(1)} %get-tuple-element.8.old_ref, f32[1,4096]{1,0:T(1,128)S(1)} %get-tuple-element.9.prior_ref), custom_call_target="tpu_custom_call" | custom-call | tf_op jit(solution)/shard_map/next_row_sums/pallas_call | solution.py:208
  65.9 0.1 collective-permute-start.7
  66.0 1.2 collective-permute-done.7
  67.1 0.1 multiply_add_fusion.2
  67.2 1.6 %collective-permute-start.8 = (f32[1,4096]{1,0:T(1,128)S(1)}, f32[1,4096]{1,0:T(1,128)S(1)}, u32[]{:S(2)}, u32[]{:S(2)}) collective-permute-start(f32[1,4096]{1,0:T(1,128)S(1)} %multiply_add_fusion.2), channel_id=1, source_target_pairs={{0,2},{2,0},{4,6},{6,4},{1,3},{3,1},{5,7},{7,5},{8,10},{10,8},{12,... | collective-permute-start | bytes 49160 | tf_op jit(solution)/shard_map/ppermute | solution.py:261
  68.8 2.2 %collective-permute-done.8 = f32[1,4096]{1,0:T(1,128)S(1)} collective-permute-done((f32[1,4096]{1,0:T(1,128)S(1)}, f32[1,4096]{1,0:T(1,128)S(1)}, u32[]{:S(2)}, u32[]{:S(2)}) %collective-permute-start.8) | collective-permute-done | bytes 16416 | tf_op jit(solution)/shard_map/ppermute | solution.py:261
  71.0 0.1 multiply_add_fusion.1
  71.1 0.0 copy-done.1
  71.1 0.3 collective-permute-start.9
  71.4 3.8 %collective-permute-done.9 = f32[1,5120]{1,0:T(1,128)S(1)} collective-permute-done((f32[1,5120]{1,0:T(1,128)S(1)}, f32[1,5120]{1,0:T(1,128)S(1)}, u32[]{:S(2)}, u32[]{:S(2)}) %collective-permute-start.9) | collective-permute-done | bytes 20512 | tf_op jit(solution)/shard_map/ppermute | solution.py:261
  75.2 0.1 multiply_add_fusion.refs_1_
  75.3 2.1 %collective-permute-start.10 = (f32[1,6144]{1,0:T(1,128)S(1)}, f32[1,6144]{1,0:T(1,128)S(1)}, u32[]{:S(2)}, u32[]{:S(2)}) collective-permute-start(f32[1,6144]{1,0:T(1,128)S(1)} %pad_maximum_fusion.5), channel_id=1, source_target_pairs={{0,96},{32,64},{64,32},{96,0},{1,97},{33,65},{65,33},{97,1},{2,98}... | collective-permute-start | bytes 73736 | tf_op jit(solution)/shard_map/ppermute | solution.py:261
  77.5 2.9 %collective-permute-done.10.refs_2_ = f32[1,6144]{1,0:T(1,128)S(1)} collective-permute-done((f32[1,6144]{1,0:T(1,128)S(1)}, f32[1,6144]{1,0:T(1,128)S(1)}, u32[]{:S(2)}, u32[]{:S(2)}) %collective-permute-start.10) | collective-permute-done | bytes 24608 | tf_op jit(solution)/shard_map/ppermute | solution.py:261
  80.4 7.5 %first_column_sums.1 = (f32[1,3072]{1,0:T(1,128)S(1)}, bf16[4096,128]{1,0:T(8,128)(2,1)S(1)}) custom-call(bf16[16,64,256]{2,1,0:T(8,128)(2,1)S(1)} %pad_maximum_fusion.s_ref.refs_0_, f32[1,4096]{1,0:T(1,128)S(1)} %multiply_add_fusion.refs_1_, f32[1,6144]{1,0:T(1,128)S(1)} %collective-permute-done.10.refs_2_, f32[1,2048]{1,0:T(1,128)S(1)} %broadcast_select_fusion.6.refs_3_, ...), custom_call_target="tpu_custom_call" | custom-call | tf_op jit(solution)/shard_map/first_column_sums/pallas_call | solution.py:208
  87.9 35.5 %collective-permute-start.11 = (f32[1,3072]{1,0:T(1,128)S(1)}, f32[1,3072]{1,0:T(1,128)S(1)}, u32[]{:S(2)}, u32[]{:S(2)}) collective-permute-start(f32[1,3072]{1,0:T(1,128)S(1)} %get-tuple-element.11), channel_id=1, source_target_pairs={{0,8},{8,0},{16,24},{24,16},{1,9},{9,1},{17,25},{25,17},{2,10},{10... | collective-permute-start | bytes 36872 | tf_op jit(solution)/shard_map/ppermute | solution.py:261
  123.4 0.1 add_reduce_fusion
  123.5 21.8 %next_column_sums.4 = f32[1,1536]{1,0:T(1,128)S(1)} custom-call(bf16[4096,128]{1,0:T(8,128)(2,1)S(1)} %get-tuple-element.10.stream_ref, bf16[4,65,768]{2,1,0:T(8,128)(2,1)S(1)} %pad_maximum_fusion.1.t_ref), custom_call_target="tpu_custom_call" | custom-call | tf_op jit(solution)/shard_map/next_column_sums/pallas_call | solution.py:208
  145.4 0.0 collective-permute-done.11
  145.4 0.1 collective-permute-start.12
  145.5 2.2 %next_column_sums.5 = f32[1,768]{1,0:T(1,128)S(1)} custom-call(bf16[4096,128]{1,0:T(8,128)(2,1)S(1)} %get-tuple-element.10.stream_ref, bf16[4,65,768]{2,1,0:T(8,128)(2,1)S(1)} %pad_maximum_fusion.1.t_ref), custom_call_target="tpu_custom_call" | custom-call | tf_op jit(solution)/shard_map/next_column_sums/pallas_call | solution.py:208
  147.7 1.4 collective-permute-done.12
  149.2 0.1 collective-permute-start.13
  149.3 0.6 multiply_subtract_fusion.1
  149.9 2.2 %next_column_sums.3 = f32[1,768]{1,0:T(1,128)S(1)} custom-call(bf16[4096,128]{1,0:T(8,128)(2,1)S(1)} %get-tuple-element.10.stream_ref, bf16[4,65,768]{2,1,0:T(8,128)(2,1)S(1)} %pad_maximum_fusion.1.t_ref), custom_call_target="tpu_custom_call" | custom-call | tf_op jit(solution)/shard_map/next_column_sums/pallas_call | solution.py:208
  152.0 0.0 copy-start.3
  152.1 2.0 %collective-permute-done.13 = f32[1,768]{1,0:T(1,128)S(1)} collective-permute-done((f32[1,768]{1,0:T(1,128)S(1)}, f32[1,768]{1,0:T(1,128)S(1)}, u32[]{:S(2)}, u32[]{:S(2)}) %collective-permute-start.13) | collective-permute-done | bytes 3104 | tf_op jit(solution)/shard_map/ppermute | solution.py:261
  154.1 0.1 multiply_reduce_fusion.2
  154.2 0.0 copy-done.3
  154.2 0.6 multiply_subtract_fusion
  (27 shorter events, 0.5 us)
Async XLA Ops:
  0.6 4.2 %collective-permute-start.3 = (bf16[1,64,256]{2,1,0:T(8,128)(2,1)}, bf16[1,64,256]{2,1,0:T(8,128)(2,1)S(1)}, u32[]{:S(2)}, u32[]{:S(2)}) collective-permute-start(bf16[1,64,256]{2,1,0:T(8,128)(2,1)} %bitcast.34), channel_id=1, source_target_pairs={{0,2},{2,0},{4,6},{6,4},{1,3},{3,1},{5,7},{7,5},{8,10},{10,8},{12,... | collective-permute-start | bytes 98312 | tf_op jit(solution)/shard_map/ppermute | solution.py:261
  2.2 0.8 copy-start.2
  2.2 4.6 %copy-start = (bf16[64,768]{1,0:T(8,128)(2,1)S(1)}, bf16[64,768]{1,0:T(8,128)(2,1)}, u32[]{:S(2)}) copy-start(bf16[64,768]{1,0:T(8,128)(2,1)} %param.6) | copy-start | bytes 294916
  3.0 3.8 %copy-start.4 = (bf16[1,768]{1,0:T(2,128)(2,1)S(1)}, bf16[1,768]{1,0:T(2,128)(2,1)}, u32[]{:S(2)}) copy-start(bf16[1,768]{1,0:T(2,128)(2,1)} %param.9) | copy-start | bytes 4612
  4.8 4.8 %collective-permute-start.4 = (bf16[2,64,256]{2,1,0:T(8,128)(2,1)S(1)}, bf16[2,64,256]{2,1,0:T(8,128)(2,1)S(1)}, u32[]{:S(2)}, u32[]{:S(2)}) collective-permute-start(bf16[2,64,256]{2,1,0:T(8,128)(2,1)S(1)} %constant_dynamic-update-slice_fusion), channel_id=1, source_target_pairs={{0,32},{32,0},{64,96},{96,64},{1,33},{33,1},{65,97},{97,65},{2,34}... | collective-permute-start | bytes 196616 | tf_op jit(solution)/shard_map/ppermute | solution.py:261
  6.8 6.5 %collective-permute-start = (bf16[1,65,768]{2,1,0:T(8,128)(2,1)S(1)}, bf16[1,65,768]{2,1,0:T(8,128)(2,1)S(1)}, u32[]{:S(2)}, u32[]{:S(2)}) collective-permute-start(bf16[1,65,768]{2,1,0:T(8,128)(2,1)S(1)} %maximum_bitcast_fusion), channel_id=1, source_target_pairs={{0,6},{2,4},{4,2},{6,0},{1,7},{3,5},{5,3},{7,1},{8,14},{10,12},{12... | collective-permute-start | bytes 299528 | tf_op jit(solution)/shard_map/ppermute | solution.py:261
  9.7 6.6 %collective-permute-start.5 = (bf16[4,64,256]{2,1,0:T(8,128)(2,1)S(1)}, bf16[4,64,256]{2,1,0:T(8,128)(2,1)S(1)}, u32[]{:S(2)}, u32[]{:S(2)}) collective-permute-start(bf16[4,64,256]{2,1,0:T(8,128)(2,1)S(1)} %pad_maximum_fusion.4), channel_id=1, source_target_pairs={{0,96},{32,64},{64,32},{96,0},{1,97},{33,65},{65,33},{97,1},{2,98}... | collective-permute-start | bytes 393224 | tf_op jit(solution)/shard_map/ppermute | solution.py:261
  13.3 6.0 %collective-permute-start.1 = (bf16[2,65,768]{2,1,0:T(8,128)(2,1)S(1)}, bf16[2,65,768]{2,1,0:T(8,128)(2,1)S(1)}, u32[]{:S(2)}, u32[]{:S(2)}) collective-permute-start(bf16[2,65,768]{2,1,0:T(8,128)(2,1)S(1)} %pad_maximum_fusion.3), channel_id=1, source_target_pairs={{0,24},{8,16},{16,8},{24,0},{1,25},{9,17},{17,9},{25,1},{2,26},{10... | collective-permute-start | bytes 599048 | tf_op jit(solution)/shard_map/ppermute | solution.py:261
  16.3 4.8 %collective-permute-start.6 = (bf16[8,64,256]{2,1,0:T(8,128)(2,1)S(1)}, bf16[8,64,256]{2,1,0:T(8,128)(2,1)S(1)}, u32[]{:S(2)}, u32[]{:S(2)}) collective-permute-start(bf16[8,64,256]{2,1,0:T(8,128)(2,1)S(1)} %pad_maximum_fusion.2), channel_id=1, source_target_pairs={{0,1},{1,0},{2,3},{3,2},{4,5},{5,4},{6,7},{7,6},{8,9},{9,8},{10,11... | collective-permute-start | bytes 786440 | tf_op jit(solution)/shard_map/ppermute | solution.py:261
  19.4 39.2 %collective-permute-start.2 = (bf16[4,65,768]{2,1,0:T(8,128)(2,1)S(1)}, bf16[4,65,768]{2,1,0:T(8,128)(2,1)S(1)}, u32[]{:S(2)}, u32[]{:S(2)}) collective-permute-start(bf16[4,65,768]{2,1,0:T(8,128)(2,1)S(1)} %pad_maximum_fusion.1.t_ref), channel_id=1, source_target_pairs={{0,8},{8,0},{16,24},{24,16},{1,9},{9,1},{17,25},{25,17},{2,10},{10... | collective-permute-start | bytes 1198088 | tf_op jit(solution)/shard_map/ppermute | solution.py:261
  65.9 1.3 collective-permute-start.7
  67.1 4.0 %copy-start.1 = (f32[1024]{0:T(1024)S(1)}, f32[1024]{0:T(1024)}, u32[]{:S(2)}) copy-start(f32[1024]{0:T(1024)} %param.7) | copy-start | bytes 12292
  67.2 3.8 %collective-permute-start.8 = (f32[1,4096]{1,0:T(1,128)S(1)}, f32[1,4096]{1,0:T(1,128)S(1)}, u32[]{:S(2)}, u32[]{:S(2)}) collective-permute-start(f32[1,4096]{1,0:T(1,128)S(1)} %multiply_add_fusion.2), channel_id=1, source_target_pairs={{0,2},{2,0},{4,6},{6,4},{1,3},{3,1},{5,7},{7,5},{8,10},{10,8},{12,... | collective-permute-start | bytes 49160 | tf_op jit(solution)/shard_map/ppermute | solution.py:261
  71.1 4.0 %collective-permute-start.9 = (f32[1,5120]{1,0:T(1,128)S(1)}, f32[1,5120]{1,0:T(1,128)S(1)}, u32[]{:S(2)}, u32[]{:S(2)}) collective-permute-start(f32[1,5120]{1,0:T(1,128)S(1)} %pad_maximum_fusion.6), channel_id=1, source_target_pairs={{0,32},{32,0},{64,96},{96,64},{1,33},{33,1},{65,97},{97,65},{2,34}... | collective-permute-start | bytes 61448 | tf_op jit(solution)/shard_map/ppermute | solution.py:261
  75.3 5.1 %collective-permute-start.10 = (f32[1,6144]{1,0:T(1,128)S(1)}, f32[1,6144]{1,0:T(1,128)S(1)}, u32[]{:S(2)}, u32[]{:S(2)}) collective-permute-start(f32[1,6144]{1,0:T(1,128)S(1)} %pad_maximum_fusion.5), channel_id=1, source_target_pairs={{0,96},{32,64},{64,32},{96,0},{1,97},{33,65},{65,33},{97,1},{2,98}... | collective-permute-start | bytes 73736 | tf_op jit(solution)/shard_map/ppermute | solution.py:261
  87.9 57.4 %collective-permute-start.11 = (f32[1,3072]{1,0:T(1,128)S(1)}, f32[1,3072]{1,0:T(1,128)S(1)}, u32[]{:S(2)}, u32[]{:S(2)}) collective-permute-start(f32[1,3072]{1,0:T(1,128)S(1)} %get-tuple-element.11), channel_id=1, source_target_pairs={{0,8},{8,0},{16,24},{24,16},{1,9},{9,1},{17,25},{25,17},{2,10},{10... | collective-permute-start | bytes 36872 | tf_op jit(solution)/shard_map/ppermute | solution.py:261
  145.4 3.7 %collective-permute-start.12 = (f32[1,1536]{1,0:T(1,128)S(1)}, f32[1,1536]{1,0:T(1,128)S(1)}, u32[]{:S(2)}, u32[]{:S(2)}) collective-permute-start(f32[1,1536]{1,0:T(1,128)S(1)} %multiply_add_fusion.3), channel_id=1, source_target_pairs={{0,24},{8,16},{16,8},{24,0},{1,25},{9,17},{17,9},{25,1},{2,26},{10... | collective-permute-start | bytes 18440 | tf_op jit(solution)/shard_map/ppermute | solution.py:261
  149.2 4.9 %collective-permute-start.13 = (f32[1,768]{1,0:T(1,128)S(1)}, f32[1,768]{1,0:T(1,128)S(1)}, u32[]{:S(2)}, u32[]{:S(2)}) collective-permute-start(f32[1,768]{1,0:T(1,128)S(1)} %multiply_add_fusion.4), channel_id=1, source_target_pairs={{0,6},{2,4},{4,2},{6,0},{1,7},{3,5},{5,3},{7,1},{8,14},{10,12},{12... | collective-permute-start | bytes 9224 | tf_op jit(solution)/shard_map/ppermute | solution.py:261
  152.0 2.1 %copy-start.3 = (f32[768]{0:T(1024)S(1)}, f32[768]{0:T(1024)}, u32[]{:S(2)}) copy-start(f32[768]{0:T(1024)} %param.8) | copy-start | bytes 9220

commit v2 on v1

--- a/solution.py
+++ b/solution.py
@@ -19,6 +19,7 @@
 row_blocks = (1024, 1024)
 column_blocks = (1024, 768)
 largest = 3e38
+smallest = 2.0**-90
 shape = (4, 4, 2, 2, 2)
 names = ("z", "y", "xh", "xl", "core")
 x = ("xh", "xl")
@@ -124,14 +125,12 @@
         return self.out_ref[...]
 
     def run(self, prior=None):
-        if prior is None:
-            self.estimate()
-
         def attempt(state):
             total = self.sums()
             if prior is not None:
                 total = total + jnp.exp2(prior - self.shift_ref[...])
-            again = jnp.logical_not(jnp.max(total) < largest)
+            in_range = jnp.logical_and(jnp.max(total) < largest, jnp.min(total) > smallest)
+            again = jnp.logical_not(in_range)
             self.out_ref[...] = self.shift_ref[...] + jnp.log2(total)
 
             @pl.when(again)
@@ -144,25 +143,30 @@
         lax.while_loop(lambda s: jnp.logical_and(s[1], s[0] < 2), attempt, (0, True))
 
 
-def fill_row_stream(t_ref, stream_ref):
+def fill_row_stream(t_ref, stream_ref, bias_ref):
     pieces, _, width = t_ref.shape
     for k in range(pieces):
         points = t_ref[k, :dim, :]
         lifted = t_ref[k, dim : dim + 1, :].astype(jnp.float32)
         wide = points.astype(jnp.float32)
         bias = scale * (lifted - jnp.sum(wide * wide, axis=0, keepdims=True))
+        bias_ref[:, k * width : (k + 1) * width] = bias
         stream_ref[k * width : (k + 1) * width, :] = streamed_features(points, bias)
 
 
-def first_row_kernel(t_ref, s_ref, out_ref, held_ref, shift_ref, stream_ref, extra_ref):
-    fill_row_stream(t_ref, stream_ref)
+def first_row_kernel(t_ref, s_ref, out_ref, held_ref, shift_ref, bias_ref, stream_ref, extra_ref):
+    fill_row_stream(t_ref, stream_ref, bias_ref)
     for k in range(s_ref.shape[0]):
         fill_held(held_ref, k * s_ref.shape[2], s_ref[k, :dim, :])
-    LogSums(stream_ref, held_ref, extra_ref, out_ref, shift_ref, row_blocks).run()
-
-
-def next_row_kernel(t_ref, held_ref, old_ref, prior_ref, out_ref, stream_ref, extra_ref, shift_ref):
-    fill_row_stream(t_ref, stream_ref)
+    sums = LogSums(stream_ref, held_ref, extra_ref, out_ref, shift_ref, row_blocks)
+    sums.estimate()
+    sums.run()
+
+
+def next_row_kernel(
+    t_ref, held_ref, old_ref, prior_ref, out_ref, bias_ref, stream_ref, extra_ref, shift_ref
+):
+    fill_row_stream(t_ref, stream_ref, bias_ref)
     shift_ref[...] = old_ref[...]
     LogSums(stream_ref, held_ref, extra_ref, out_ref, shift_ref, row_blocks).run(prior_ref[...])
 
@@ -183,21 +187,23 @@
         stream_ref[cols, :] = streamed_features(s_ref[k], bias)
 
 
-def columns(first, t_ref, out_ref, stream_ref, held_ref, extra_ref, shift_ref):
+def columns(first, t_ref, bias_ref, out_ref, stream_ref, held_ref, extra_ref, shift_ref):
     width = t_ref.shape[2]
+    start = first * width
+    shift_ref[...] = rounded(-bias_ref[:, start : start + held_ref.shape[1]])
     for k in range(held_ref.shape[1] // width):
         fill_held(held_ref, k * width, t_ref[first + k, :dim, :])
     LogSums(stream_ref, held_ref, extra_ref, out_ref, shift_ref, column_blocks).run()
 
 
 def first_column_kernel(*refs):
-    ins, (t_ref, out_ref, stream_ref), scratch = refs[:-6], refs[-6:-3], refs[-3:]
+    ins, (t_ref, bias_ref, out_ref, stream_ref), scratch = refs[:-7], refs[-7:-3], refs[-3:]
     fill_column_stream(*ins, stream_ref)
-    columns(0, t_ref, out_ref, stream_ref, *scratch)
-
-
-def next_column_kernel(first, stream_ref, t_ref, out_ref, *scratch):
-    columns(first, t_ref, out_ref, stream_ref, *scratch)
+    columns(0, t_ref, bias_ref, out_ref, stream_ref, *scratch)
+
+
+def next_column_kernel(first, stream_ref, t_ref, bias_ref, out_ref, *scratch):
+    columns(first, t_ref, bias_ref, out_ref, stream_ref, *scratch)
 
 
 whole = pl.BlockSpec(memory_space=pltpu.VMEM)
@@ -231,29 +237,31 @@
 
 def first_row_sums(targets, sources):
     row, held, extra = arrays_of(points_of(sources))
-    outs = (row, held, row)
+    outs = (row, held, row, arrays_of(points_of(targets))[0])
     scratch = (stream_of(points_of(targets)), extra)
     return call(first_row_kernel, "first_row_sums", (targets, sources), outs, scratch)
 
 
 def next_row_sums(targets, prior, held, shift):
     row, _, extra = arrays_of(held.shape[1])
+    outs = (row, arrays_of(points_of(targets))[0])
     scratch = (stream_of(points_of(targets)), extra, row)
-    return call(next_row_kernel, "next_row_sums", (targets, held, shift, prior), (row,), scratch)[0]
-
-
-def first_column_sums(targets, sources, *more):
+    return call(next_row_kernel, "next_row_sums", (targets, held, shift, prior), outs, scratch)
+
+
+def first_column_sums(targets, biases, sources, *more):
     row, held, extra = arrays_of(points_of(targets))
-    operands = (sources, *more, targets)
+    operands = (sources, *more, targets, biases)
     specs = [scalar if v.dtype == jnp.int32 else whole for v in operands]
     outs = (row, stream_of(points_of(sources)))
     return call(first_column_kernel, "first_column_sums", operands, outs, (held, extra, row), specs)
 
 
-def next_column_sums(stream, targets, first, count):
+def next_column_sums(stream, targets, biases, first, count):
     row, held, extra = arrays_of(count * targets.shape[2])
     kernel = functools.partial(next_column_kernel, first)
-    return call(kernel, "next_column_sums", (stream, targets), (row,), (held, extra, row))[0]
+    operands = (stream, targets, biases)
+    return call(kernel, "next_column_sums", operands, (row,), (held, extra, row))[0]
 
 
 def exchange(v, axes, flip):
@@ -292,9 +300,11 @@
     sources = doubled(sources, "core", 1, core)
     others = exchange(targets, "y", 1)
 
-    lse, held, shift = first_row_sums(targets, sources)
-    lse = next_row_sums(others, lse, held, shift)
+    lse, held, shift, biases = first_row_sums(targets, sources)
+    lse, other_biases = next_row_sums(others, lse, held, shift)
     lse = log_add(lse, exchange(lse, "core", 1))
+    column_base = smoothing * target_logw
+    lse, column_base = lax.optimization_barrier((lse, column_base))
     lse = log_add(lse, exchange(lse, x, 1))
     count = lse.shape[1]
     logw = source_logw[None]
@@ -308,17 +318,17 @@
     )
     received = exchange(jnp.concatenate([lse, logw], axis=1), "z", 3)
     place = (z // 2).astype(jnp.int32).reshape(1)
-    partial, stream = first_column_sums(others, sources, lse, received, logw, place)
+    partial, stream = first_column_sums(others, other_biases, sources, lse, received, logw, place)
 
     sent = exchange(partial, "y", 1)
     half = 2 * span
-    partial = next_column_sums(stream, targets, 2, 2)
+    partial = next_column_sums(stream, targets, biases, 2, 2)
     partial = log_add(partial, sent[:, half:])
     more = exchange(partial, "y", 3)
-    partial = next_column_sums(stream, targets, 1, 1)
+    partial = next_column_sums(stream, targets, biases, 1, 1)
     partial = log_add(log_add(partial, sent[:, span:half]), more[:, span:])
     last = exchange(partial, x, 3)
-    partial = next_column_sums(stream, targets, 0, 1)
+    partial = next_column_sums(stream, targets, biases, 0, 1)
     partial = log_add(log_add(partial, sent[:, :span]), more[:, :span])
     partial = log_add(partial, last)[0]
 
@@ -334,7 +344,7 @@
     row_potential = smoothing * source_logw - smoothing * row_lse
 
     col_lse = partial / log2e - norms(target) / smoothing
-    col_potential = smoothing * target_logw - smoothing * col_lse
+    col_potential = column_base - smoothing * col_lse
     return (row_potential, col_potential)
 
 

time: 158 us -> 176 us (1.11)
  Pallas kernels: 78.3 us -> 131 us
  starting transfers between devices: 53.2 us -> 22.9 us
  waiting for transfers between devices: 19.5 us -> 16.1 us
    pallas_call x6, Pallas kernels: 78.3 us -> 131 us  [call(): pl.pallas_call(kernel, in_specs=in_specs or [whole] * len(operands), out_...]
    ppermute x14, starting transfers between devices: 53.2 us -> 22.9 us  [exchange(): return lax.ppermute(v, axes, [(i, i ^ flip) for i in range(size)])]
    ppermute x14, waiting for transfers between devices: 19.5 us -> 16.1 us  [exchange(): return lax.ppermute(v, axes, [(i, i ^ flip) for i in range(size)])]
  transfers between devices with their start and end apart: 14 -> 14, of which waited for: 9 -> 7; matrix products, arithmetic and copies ran while one was open for 1% -> 1% of each run, Pallas kernels for 41% -> 47%
where the time goes in v2:
time: 176 us; the launch traced here: 174 us
  Pallas kernels  131 us (74%)
  starting transfers between devices  22.9 us (13%)
  waiting for transfers between devices  16.1 us (9%)
  other arithmetic  2.02 us (1%)
    pallas_call x6, Pallas kernels, call(): pl.pallas_call(kernel, in_specs=in_specs or [whole] * len(operands), out_...  131 us
    ppermute x14, starting transfers between devices, exchange(): return lax.ppermute(v, axes, [(i, i ^ flip) for i in range(size)])  22.9 us
    ppermute x14, waiting for transfers between devices, exchange(): return lax.ppermute(v, axes, [(i, i ^ flip) for i in range(size)])  16.1 us
  transfers between devices with their start and end apart: 14, of which 7 were waited for; matrix products, arithmetic and copies ran while one was open for 1% of the time, Pallas kernels for 47%

profile of v2, /device:TPU:8, one launch (start us, length us, event | category | flops | bytes accessed | tf_op | source)
XLA Modules:
  0.0 173.5 jit_solution(1174892870016082716)
XLA Ops:
  0.6 1.6 collective-permute-start.3
  2.2 0.0 copy-start.2
  2.2 0.8 copy-done.2
  3.0 1.8 %collective-permute-done.3 = bf16[1,64,256]{2,1,0:T(8,128)(2,1)S(1)} collective-permute-done((bf16[1,64,256]{2,1,0:T(8,128)(2,1)}, bf16[1,64,256]{2,1,0:T(8,128)(2,1)S(1)}, u32[]{:S(2)}, u32[]{:S(2)}) %collective-permute-start.3) | collective-permute-done | bytes 32800 | tf_op jit(solution)/shard_map/ppermute | solution.py:269
  4.8 1.9 %collective-permute-start.4 = (bf16[2,64,256]{2,1,0:T(8,128)(2,1)S(1)}, bf16[2,64,256]{2,1,0:T(8,128)(2,1)S(1)}, u32[]{:S(2)}, u32[]{:S(2)}) collective-permute-start(bf16[2,64,256]{2,1,0:T(8,128)(2,1)S(1)} %constant_dynamic-update-slice_fusion), channel_id=1, source_target_pairs={{0,32},{32,0},{64,96},{96,64},{1,33},{33,1},{65,97},{97,65},{2,34}... | collective-permute-start | bytes 196616 | tf_op jit(solution)/shard_map/ppermute | solution.py:269
  6.8 0.0 copy-done
  6.8 0.0 copy-done.4
  6.8 2.8 %collective-permute-start = (bf16[1,65,768]{2,1,0:T(8,128)(2,1)S(1)}, bf16[1,65,768]{2,1,0:T(8,128)(2,1)S(1)}, u32[]{:S(2)}, u32[]{:S(2)}) collective-permute-start(bf16[1,65,768]{2,1,0:T(8,128)(2,1)S(1)} %maximum_bitcast_fusion), channel_id=1, source_target_pairs={{0,6},{2,4},{4,2},{6,0},{1,7},{3,5},{5,3},{7,1},{8,14},{10,12},{12... | collective-permute-start | bytes 299528 | tf_op jit(solution)/shard_map/ppermute | solution.py:269
  9.6 0.0 collective-permute-done.4
  9.7 3.6 %collective-permute-start.5 = (bf16[4,64,256]{2,1,0:T(8,128)(2,1)S(1)}, bf16[4,64,256]{2,1,0:T(8,128)(2,1)S(1)}, u32[]{:S(2)}, u32[]{:S(2)}) collective-permute-start(bf16[4,64,256]{2,1,0:T(8,128)(2,1)S(1)} %pad_maximum_fusion.4), channel_id=1, source_target_pairs={{0,96},{32,64},{64,32},{96,0},{1,97},{33,65},{65,33},{97,1},{2,98}... | collective-permute-start | bytes 393224 | tf_op jit(solution)/shard_map/ppermute | solution.py:269
  13.3 0.0 collective-permute-done
  13.3 1.7 collective-permute-start.1
  14.9 1.3 collective-permute-done.5
  16.3 0.1 collective-permute-start.6
  16.4 2.9 %collective-permute-done.1 = bf16[2,65,768]{2,1,0:T(8,128)(2,1)S(1)} collective-permute-done((bf16[2,65,768]{2,1,0:T(8,128)(2,1)S(1)}, bf16[2,65,768]{2,1,0:T(8,128)(2,1)S(1)}, u32[]{:S(2)}, u32[]{:S(2)}) %collective-permute-start.1) | collective-permute-done | bytes 199712 | tf_op jit(solution)/shard_map/ppermute | solution.py:269
  19.4 1.7 %collective-permute-start.2 = (bf16[4,65,768]{2,1,0:T(8,128)(2,1)S(1)}, bf16[4,65,768]{2,1,0:T(8,128)(2,1)S(1)}, u32[]{:S(2)}, u32[]{:S(2)}) collective-permute-start(bf16[4,65,768]{2,1,0:T(8,128)(2,1)S(1)} %pad_maximum_fusion.1.t_ref), channel_id=1, source_target_pairs={{0,8},{8,0},{16,24},{24,16},{1,9},{9,1},{17,25},{25,17},{2,10},{10... | collective-permute-start | bytes 1198088 | tf_op jit(solution)/shard_map/ppermute | solution.py:269
  21.1 0.0 collective-permute-done.6
  21.2 37.3 %first_row_sums.1 = (f32[1,4096]{1,0:T(1,128)S(1)}, bf16[128,4096]{1,0:T(8,128)(2,1)S(1)}, f32[1,4096]{1,0:T(1,128)S(1)}, f32[1,3072]{1,0:T(1,128)S(1)}) custom-call(bf16[4,65,768]{2,1,0:T(8,128)(2,1)S(1)} %pad_maximum_fusion.1.t_ref, bf16[16,64,256]{2,1,0:T(8,128)(2,1)S(1)} %pad_maximum_fusion.s_ref.refs_0_), custom_call_target="tpu_custom_call" | custom-call | tf_op jit(solution)/shard_map/first_row_sums/pallas_call | solution.py:214
  58.6 0.0 collective-permute-done.2.t_ref.refs_5_
  58.6 0.0 copy-start.3
  58.6 7.3 %next_row_sums.1 = (f32[1,4096]{1,0:T(1,128)S(1)}, f32[1,3072]{1,0:T(1,128)S(1)}) custom-call(bf16[4,65,768]{2,1,0:T(8,128)(2,1)S(1)} %collective-permute-done.2.t_ref.refs_5_, bf16[128,4096]{1,0:T(8,128)(2,1)S(1)} %get-tuple-element.12.held_ref, f32[1,4096]{1,0:T(1,128)S(1)} %get-tuple-element.13.old_ref, f32[1,4096]{1,0:T(1,128)S(1)} %get-tuple-element.14.prior_ref), custom_call_target="tpu_custom_call" | custom-call | tf_op jit(solution)/shard_map/next_row_sums/pallas_call | solution.py:214
  65.9 0.1 collective-permute-start.7
  66.0 0.0 copy-done.3
  66.0 1.1 collective-permute-done.7
  67.2 0.1 multiply_add_fusion.2
  67.2 1.6 collective-permute-start.8
  68.8 2.2 %collective-permute-done.8 = f32[1,4096]{1,0:T(1,128)S(1)} collective-permute-done((f32[1,4096]{1,0:T(1,128)S(1)}, f32[1,4096]{1,0:T(1,128)S(1)}, u32[]{:S(2)}, u32[]{:S(2)}) %collective-permute-start.8) | collective-permute-done | bytes 16416 | tf_op jit(solution)/shard_map/ppermute | solution.py:269
  71.1 0.1 multiply_add_fusion.1
  71.1 0.0 copy-done.1
  71.2 0.3 collective-permute-start.9
  71.5 3.8 %collective-permute-done.9 = f32[1,5120]{1,0:T(1,128)S(1)} collective-permute-done((f32[1,5120]{1,0:T(1,128)S(1)}, f32[1,5120]{1,0:T(1,128)S(1)}, u32[]{:S(2)}, u32[]{:S(2)}) %collective-permute-start.9) | collective-permute-done | bytes 20512 | tf_op jit(solution)/shard_map/ppermute | solution.py:269
  75.2 0.1 multiply_add_fusion.refs_1_
  75.3 2.2 %collective-permute-start.10 = (f32[1,6144]{1,0:T(1,128)S(1)}, f32[1,6144]{1,0:T(1,128)S(1)}, u32[]{:S(2)}, u32[]{:S(2)}) collective-permute-start(f32[1,6144]{1,0:T(1,128)S(1)} %pad_maximum_fusion.5), channel_id=1, source_target_pairs={{0,96},{32,64},{64,32},{96,0},{1,97},{33,65},{65,33},{97,1},{2,98}... | collective-permute-start | bytes 73736 | tf_op jit(solution)/shard_map/ppermute | solution.py:269
  77.6 2.9 %collective-permute-done.10.refs_2_ = f32[1,6144]{1,0:T(1,128)S(1)} collective-permute-done((f32[1,6144]{1,0:T(1,128)S(1)}, f32[1,6144]{1,0:T(1,128)S(1)}, u32[]{:S(2)}, u32[]{:S(2)}) %collective-permute-start.10) | collective-permute-done | bytes 24608 | tf_op jit(solution)/shard_map/ppermute | solution.py:269
  80.5 42.6 %first_column_sums.1 = (f32[1,3072]{1,0:T(1,128)S(1)}, bf16[4096,128]{1,0:T(8,128)(2,1)S(1)}) custom-call(bf16[16,64,256]{2,1,0:T(8,128)(2,1)S(1)} %pad_maximum_fusion.s_ref.refs_0_, f32[1,4096]{1,0:T(1,128)S(1)} %multiply_add_fusion.refs_1_, f32[1,6144]{1,0:T(1,128)S(1)} %collective-permute-done.10.refs_2_, f32[1,2048]{1,0:T(1,128)S(1)} %broadcast_select_fusion.6.refs_3_, ...), custom_call_target="tpu_custom_call" | custom-call | tf_op jit(solution)/shard_map/first_column_sums/pallas_call | solution.py:214
  123.0 0.1 collective-permute-start.11
  123.1 0.1 add_reduce_fusion
  123.2 21.6 %next_column_sums.4 = f32[1,1536]{1,0:T(1,128)S(1)} custom-call(bf16[4096,128]{1,0:T(8,128)(2,1)S(1)} %get-tuple-element.19.stream_ref, bf16[4,65,768]{2,1,0:T(8,128)(2,1)S(1)} %pad_maximum_fusion.1.t_ref, f32[1,3072]{1,0:T(1,128)S(1)} %get-tuple-element.20.bias_ref), custom_call_target="tpu_custom_call" | custom-call | tf_op jit(solution)/shard_map/next_column_sums/pallas_call | solution.py:214
  144.9 0.0 collective-permute-done.11
  144.9 2.5 %collective-permute-start.12 = (f32[1,1536]{1,0:T(1,128)S(1)}, f32[1,1536]{1,0:T(1,128)S(1)}, u32[]{:S(2)}, u32[]{:S(2)}) collective-permute-start(f32[1,1536]{1,0:T(1,128)S(1)} %multiply_add_fusion.3), channel_id=1, source_target_pairs={{0,24},{8,16},{16,8},{24,0},{1,25},{9,17},{17,9},{25,1},{2,26},{10... | collective-permute-start | bytes 18440 | tf_op jit(solution)/shard_map/ppermute | solution.py:269
  147.4 10.9 %next_column_sums.5 = f32[1,768]{1,0:T(1,128)S(1)} custom-call(bf16[4096,128]{1,0:T(8,128)(2,1)S(1)} %get-tuple-element.19.stream_ref, bf16[4,65,768]{2,1,0:T(8,128)(2,1)S(1)} %pad_maximum_fusion.1.t_ref, f32[1,3072]{1,0:T(1,128)S(1)} %get-tuple-element.20.bias_ref), custom_call_target="tpu_custom_call" | custom-call | tf_op jit(solution)/shard_map/next_column_sums/pallas_call | solution.py:214
  158.4 0.0 collective-permute-done.12
  158.4 2.8 %collective-permute-start.13 = (f32[1,768]{1,0:T(1,128)S(1)}, f32[1,768]{1,0:T(1,128)S(1)}, u32[]{:S(2)}, u32[]{:S(2)}) collective-permute-start(f32[1,768]{1,0:T(1,128)S(1)} %multiply_add_fusion.4), channel_id=1, source_target_pairs={{0,6},{2,4},{4,2},{6,0},{1,7},{3,5},{5,3},{7,1},{8,14},{10,12},{12... | collective-permute-start | bytes 9224 | tf_op jit(solution)/shard_map/ppermute | solution.py:269
  161.3 0.6 multiply_subtract_fusion.1
  161.9 10.9 %next_column_sums.3 = f32[1,768]{1,0:T(1,128)S(1)} custom-call(bf16[4096,128]{1,0:T(8,128)(2,1)S(1)} %get-tuple-element.19.stream_ref, bf16[4,65,768]{2,1,0:T(8,128)(2,1)S(1)} %pad_maximum_fusion.1.t_ref, f32[1,3072]{1,0:T(1,128)S(1)} %get-tuple-element.20.bias_ref), custom_call_target="tpu_custom_call" | custom-call | tf_op jit(solution)/shard_map/next_column_sums/pallas_call | solution.py:214
  172.8 0.0 collective-permute-done.13
  172.8 0.1 multiply_reduce_fusion.2
  172.9 0.6 multiply_subtract_fusion
  (28 shorter events, 0.5 us)
Async XLA Ops:
  0.6 4.2 %collective-permute-start.3 = (bf16[1,64,256]{2,1,0:T(8,128)(2,1)}, bf16[1,64,256]{2,1,0:T(8,128)(2,1)S(1)}, u32[]{:S(2)}, u32[]{:S(2)}) collective-permute-start(bf16[1,64,256]{2,1,0:T(8,128)(2,1)} %bitcast.34), channel_id=1, source_target_pairs={{0,2},{2,0},{4,6},{6,4},{1,3},{3,1},{5,7},{7,5},{8,10},{10,8},{12,... | collective-permute-start | bytes 98312 | tf_op jit(solution)/shard_map/ppermute | solution.py:269
  2.2 0.8 copy-start.2
  2.2 4.6 %copy-start = (bf16[64,768]{1,0:T(8,128)(2,1)S(1)}, bf16[64,768]{1,0:T(8,128)(2,1)}, u32[]{:S(2)}) copy-start(bf16[64,768]{1,0:T(8,128)(2,1)} %param.6) | copy-start | bytes 294916
  3.0 3.8 %copy-start.4 = (bf16[1,768]{1,0:T(2,128)(2,1)S(1)}, bf16[1,768]{1,0:T(2,128)(2,1)}, u32[]{:S(2)}) copy-start(bf16[1,768]{1,0:T(2,128)(2,1)} %param.9) | copy-start | bytes 4612
  4.8 4.8 %collective-permute-start.4 = (bf16[2,64,256]{2,1,0:T(8,128)(2,1)S(1)}, bf16[2,64,256]{2,1,0:T(8,128)(2,1)S(1)}, u32[]{:S(2)}, u32[]{:S(2)}) collective-permute-start(bf16[2,64,256]{2,1,0:T(8,128)(2,1)S(1)} %constant_dynamic-update-slice_fusion), channel_id=1, source_target_pairs={{0,32},{32,0},{64,96},{96,64},{1,33},{33,1},{65,97},{97,65},{2,34}... | collective-permute-start | bytes 196616 | tf_op jit(solution)/shard_map/ppermute | solution.py:269
  6.8 6.5 %collective-permute-start = (bf16[1,65,768]{2,1,0:T(8,128)(2,1)S(1)}, bf16[1,65,768]{2,1,0:T(8,128)(2,1)S(1)}, u32[]{:S(2)}, u32[]{:S(2)}) collective-permute-start(bf16[1,65,768]{2,1,0:T(8,128)(2,1)S(1)} %maximum_bitcast_fusion), channel_id=1, source_target_pairs={{0,6},{2,4},{4,2},{6,0},{1,7},{3,5},{5,3},{7,1},{8,14},{10,12},{12... | collective-permute-start | bytes 299528 | tf_op jit(solution)/shard_map/ppermute | solution.py:269
  9.7 6.6 %collective-permute-start.5 = (bf16[4,64,256]{2,1,0:T(8,128)(2,1)S(1)}, bf16[4,64,256]{2,1,0:T(8,128)(2,1)S(1)}, u32[]{:S(2)}, u32[]{:S(2)}) collective-permute-start(bf16[4,64,256]{2,1,0:T(8,128)(2,1)S(1)} %pad_maximum_fusion.4), channel_id=1, source_target_pairs={{0,96},{32,64},{64,32},{96,0},{1,97},{33,65},{65,33},{97,1},{2,98}... | collective-permute-start | bytes 393224 | tf_op jit(solution)/shard_map/ppermute | solution.py:269
  13.3 6.0 %collective-permute-start.1 = (bf16[2,65,768]{2,1,0:T(8,128)(2,1)S(1)}, bf16[2,65,768]{2,1,0:T(8,128)(2,1)S(1)}, u32[]{:S(2)}, u32[]{:S(2)}) collective-permute-start(bf16[2,65,768]{2,1,0:T(8,128)(2,1)S(1)} %pad_maximum_fusion.3), channel_id=1, source_target_pairs={{0,24},{8,16},{16,8},{24,0},{1,25},{9,17},{17,9},{25,1},{2,26},{10... | collective-permute-start | bytes 599048 | tf_op jit(solution)/shard_map/ppermute | solution.py:269
  16.3 4.8 %collective-permute-start.6 = (bf16[8,64,256]{2,1,0:T(8,128)(2,1)S(1)}, bf16[8,64,256]{2,1,0:T(8,128)(2,1)S(1)}, u32[]{:S(2)}, u32[]{:S(2)}) collective-permute-start(bf16[8,64,256]{2,1,0:T(8,128)(2,1)S(1)} %pad_maximum_fusion.2), channel_id=1, source_target_pairs={{0,1},{1,0},{2,3},{3,2},{4,5},{5,4},{6,7},{7,6},{8,9},{9,8},{10,11... | collective-permute-start | bytes 786440 | tf_op jit(solution)/shard_map/ppermute | solution.py:269
  19.4 39.2 %collective-permute-start.2 = (bf16[4,65,768]{2,1,0:T(8,128)(2,1)S(1)}, bf16[4,65,768]{2,1,0:T(8,128)(2,1)S(1)}, u32[]{:S(2)}, u32[]{:S(2)}) collective-permute-start(bf16[4,65,768]{2,1,0:T(8,128)(2,1)S(1)} %pad_maximum_fusion.1.t_ref), channel_id=1, source_target_pairs={{0,8},{8,0},{16,24},{24,16},{1,9},{9,1},{17,25},{25,17},{2,10},{10... | collective-permute-start | bytes 1198088 | tf_op jit(solution)/shard_map/ppermute | solution.py:269
  58.6 7.4 %copy-start.3 = (f32[768]{0:T(1024)S(1)}, f32[768]{0:T(1024)}, u32[]{:S(2)}) copy-start(f32[768]{0:T(1024)} %param.8) | copy-start | bytes 9220
  65.9 1.3 collective-permute-start.7
  67.2 4.0 %copy-start.1 = (f32[1024]{0:T(1024)S(1)}, f32[1024]{0:T(1024)}, u32[]{:S(2)}) copy-start(f32[1024]{0:T(1024)} %param.7) | copy-start | bytes 12292
  67.2 3.8 %collective-permute-start.8 = (f32[1,4096]{1,0:T(1,128)S(1)}, f32[1,4096]{1,0:T(1,128)S(1)}, u32[]{:S(2)}, u32[]{:S(2)}) collective-permute-start(f32[1,4096]{1,0:T(1,128)S(1)} %multiply_add_fusion.2), channel_id=1, source_target_pairs={{0,2},{2,0},{4,6},{6,4},{1,3},{3,1},{5,7},{7,5},{8,10},{10,8},{12,... | collective-permute-start | bytes 49160 | tf_op jit(solution)/shard_map/ppermute | solution.py:269
  71.2 4.0 %collective-permute-start.9 = (f32[1,5120]{1,0:T(1,128)S(1)}, f32[1,5120]{1,0:T(1,128)S(1)}, u32[]{:S(2)}, u32[]{:S(2)}) collective-permute-start(f32[1,5120]{1,0:T(1,128)S(1)} %pad_maximum_fusion.6), channel_id=1, source_target_pairs={{0,32},{32,0},{64,96},{96,64},{1,33},{33,1},{65,97},{97,65},{2,34}... | collective-permute-start | bytes 61448 | tf_op jit(solution)/shard_map/ppermute | solution.py:269
  75.3 5.1 %collective-permute-start.10 = (f32[1,6144]{1,0:T(1,128)S(1)}, f32[1,6144]{1,0:T(1,128)S(1)}, u32[]{:S(2)}, u32[]{:S(2)}) collective-permute-start(f32[1,6144]{1,0:T(1,128)S(1)} %pad_maximum_fusion.5), channel_id=1, source_target_pairs={{0,96},{32,64},{64,32},{96,0},{1,97},{33,65},{65,33},{97,1},{2,98}... | collective-permute-start | bytes 73736 | tf_op jit(solution)/shard_map/ppermute | solution.py:269
  123.0 21.8 %collective-permute-start.11 = (f32[1,3072]{1,0:T(1,128)S(1)}, f32[1,3072]{1,0:T(1,128)S(1)}, u32[]{:S(2)}, u32[]{:S(2)}) collective-permute-start(f32[1,3072]{1,0:T(1,128)S(1)} %get-tuple-element.21), channel_id=1, source_target_pairs={{0,8},{8,0},{16,24},{24,16},{1,9},{9,1},{17,25},{25,17},{2,10},{10... | collective-permute-start | bytes 36872 | tf_op jit(solution)/shard_map/ppermute | solution.py:269
  144.9 13.5 %collective-permute-start.12 = (f32[1,1536]{1,0:T(1,128)S(1)}, f32[1,1536]{1,0:T(1,128)S(1)}, u32[]{:S(2)}, u32[]{:S(2)}) collective-permute-start(f32[1,1536]{1,0:T(1,128)S(1)} %multiply_add_fusion.3), channel_id=1, source_target_pairs={{0,24},{8,16},{16,8},{24,0},{1,25},{9,17},{17,9},{25,1},{2,26},{10... | collective-permute-start | bytes 18440 | tf_op jit(solution)/shard_map/ppermute | solution.py:269
  158.4 14.4 %collective-permute-start.13 = (f32[1,768]{1,0:T(1,128)S(1)}, f32[1,768]{1,0:T(1,128)S(1)}, u32[]{:S(2)}, u32[]{:S(2)}) collective-permute-start(f32[1,768]{1,0:T(1,128)S(1)} %multiply_add_fusion.4), channel_id=1, source_target_pairs={{0,6},{2,4},{4,2},{6,0},{1,7},{3,5},{5,3},{7,1},{8,14},{10,12},{12... | collective-permute-start | bytes 9224 | tf_op jit(solution)/shard_map/ppermute | solution.py:269
